TPU v7x, 32 devices: a whole 2x2x4 slice. The times are simulated.
32 devices in a mesh: dp: 16 (over z, y, x), tensor: 2 (over core).
Axes of the slice: x: 2, y: 2, z: 4, core: 2. Of those that a mesh axis runs over, the one named last changes fastest.
Arguments:
- tokens: bfloat16 [32, 580, 1024], P('dp', 'tensor'), may hold values from -6 to 6
- lengths: int32 [32], P('dp'), may hold values from 290 to 580, as said below
- ln1_gain: bfloat16 [1024], P('dp'), may hold values from 0.5 to 1.5
- ln1_bias: bfloat16 [1024], P('dp'), may hold values from -3 to 3
- qkv_weight: bfloat16 [1024, 3072], P('dp', 'tensor'), may hold values from -0.1875 to 0.1875
- qv_bias: bfloat16 [16, 128], P('tensor', 'dp'), may hold values from -3 to 3
- out_weight: bfloat16 [1024, 1024], P('dp', 'tensor'), may hold values from -1.5 to 1.5
- out_bias: bfloat16 [1024], P('dp'), may hold values from -3 to 3
- ln2_gain: bfloat16 [1024], P('dp'), may hold values from 0.5 to 1.5
- ln2_bias: bfloat16 [1024], P('dp'), may hold values from -3 to 3
- fc1_weight: bfloat16 [1024, 4096], P('dp', 'tensor'), may hold values from -0.1875 to 0.1875
- fc1_bias: bfloat16 [32, 128], P('tensor', 'dp'), may hold values from -3 to 3
- fc2_weight: bfloat16 [1024, 4096], P('dp', 'tensor'), may hold values from -0.09375 to 0.09375
- fc2_bias: bfloat16 [1024], P('dp'), may hold values from -3 to 3
- cotangent: bfloat16 [32, 580, 1024], P('dp', 'tensor'), may hold values from -6 to 6
Outputs:
- result: bfloat16 [32, 580, 1024], P('dp', 'tensor')
- tokens_grad: bfloat16 [32, 580, 1024], P('dp', 'tensor')
- ln1_gain_grad: float32 [1024], P('dp')
- ln1_bias_grad: float32 [1024], P('dp')
- qkv_weight_grad: float32 [1024, 3072], P('dp', 'tensor')
- qv_bias_grad: float32 [16, 128], P('tensor', 'dp')
- out_weight_grad: float32 [1024, 1024], P('dp', 'tensor')
- out_bias_grad: float32 [1024], P('dp')
- ln2_gain_grad: float32 [1024], P('dp')
- ln2_bias_grad: float32 [1024], P('dp')
- fc1_weight_grad: float32 [1024, 4096], P('dp', 'tensor')
- fc1_bias_grad: float32 [32, 128], P('tensor', 'dp')
- fc2_weight_grad: float32 [1024, 4096], P('dp', 'tensor')
- fc2_bias_grad: float32 [1024], P('dp')
Inputs may be any that keep to these rules, and one draw needn't show every extreme that they name: `lengths`: keys at positions of an image's length or beyond are masked; some image has all 580 token slots valid in every draw.
All inputs are finite; a program needn't handle non-finite values.
Results may differ from a plain program's by a relative error of at most 0.015.
Values may be sent and summed in bfloat16 or wider, within the bound.
A program may use at most 256 MiB of HBM per device.

v0:
```python
import jax
import jax.numpy as jnp
from jax import lax
from jax.sharding import PartitionSpec as P

HD = 64
MICRO = 2


def layer_stats(values):
    center = values - jnp.mean(values, -1, keepdims=True)
    inverse = lax.rsqrt(jnp.mean(center * center, -1, keepdims=True) + 1e-05)
    return (center * inverse, inverse)


def stats_backward(grad_norm, normed, inverse, gain):
    scaled = grad_norm * gain
    return inverse * (
        scaled
        - jnp.mean(scaled, -1, keepdims=True)
        - normed * jnp.mean(scaled * normed, -1, keepdims=True)
    )


def contract_last(left, right):
    return lax.dot_general(
        left, right, (((2,), (1,)), ((), ())), preferred_element_type=jnp.float32
    )


def row_total(values):
    return jnp.sum(values, axis=(0, 1))


def to_heads(packed, heads_local):
    batch, length, width = packed.shape
    return jnp.moveaxis(packed.reshape(batch, length, heads_local, width // heads_local), 2, 0)


def from_heads(stacked):
    heads_local, batch, length, width = stacked.shape
    return jnp.moveaxis(stacked, 0, 2).reshape(batch, length, heads_local * width)


def masked_scores(query_matrix, key_matrix_rows, key_mask):
    scores = jnp.einsum(
        "xjz,xez->xje", query_matrix, key_matrix_rows, preferred_element_type=jnp.float32
    ) * HD ** (-0.5)
    return jnp.where(key_mask, scores, -1e30)


def body(
    tokens,
    lengths,
    ln1_gain,
    ln1_bias,
    qkv_weight,
    qv_bias,
    out_weight,
    out_bias,
    ln2_gain,
    ln2_bias,
    fc1_weight,
    fc1_bias,
    fc2_weight,
    fc2_bias,
    cotangent,
):
    per_micro = tokens.shape[0] // MICRO
    heads_local = qv_bias.shape[0]
    seq_full = tokens.shape[1] * lax.axis_size("tensor")
    totals = None
    out_parts = []
    grad_parts = []
    for micro_idx in range(MICRO):
        weights_now = (
            lax.all_gather(qkv_weight, "dp", axis=0, tiled=True),
            lax.all_gather(out_weight, "dp", axis=0, tiled=True),
            lax.all_gather(fc1_weight, "dp", axis=0, tiled=True),
            lax.all_gather(fc2_weight, "dp", axis=0, tiled=True),
            lax.all_gather(qv_bias, "dp", axis=1, tiled=True),
            lax.all_gather(fc1_bias, "dp", axis=1, tiled=True),
            lax.all_gather(ln1_gain, "dp", axis=0, tiled=True),
            lax.all_gather(ln1_bias, "dp", axis=0, tiled=True),
            lax.all_gather(out_bias, "dp", axis=0, tiled=True),
            lax.all_gather(ln2_gain, "dp", axis=0, tiled=True),
            lax.all_gather(ln2_bias, "dp", axis=0, tiled=True),
            lax.all_gather(fc2_bias, "dp", axis=0, tiled=True),
        )
        (
            w_qkv,
            w_out,
            w_fc1,
            w_fc2,
            qv_full,
            fc1_full,
            gain_one,
            shift_one,
            out_shift,
            gain_two,
            shift_two,
            fc2_shift,
        ) = weights_now
        qv_shift = qv_full.astype(jnp.float32)
        fc1_shift = fc1_full.astype(jnp.float32).reshape(-1)
        gain_one = gain_one.astype(jnp.float32)
        shift_one = shift_one.astype(jnp.float32)
        out_shift = out_shift.astype(jnp.float32)
        gain_two = gain_two.astype(jnp.float32)
        shift_two = shift_two.astype(jnp.float32)
        fc2_shift = fc2_shift.astype(jnp.float32)
        window = slice(micro_idx * per_micro, (micro_idx + 1) * per_micro)
        token_rows = tokens[window].astype(jnp.float32)
        cot_low = cotangent[window]
        image_lengths = lengths[window]
        key_mask = (
            jnp.arange(seq_full, dtype=jnp.int32)[None, None, :] < image_lengths[:, None, None]
        )
        normed_one, inverse_one = layer_stats(token_rows)
        hidden_one = (normed_one * gain_one + shift_one).astype(jnp.bfloat16)
        hidden_one_full = lax.all_gather(hidden_one, "tensor", axis=1, tiled=True)
        no_key_bias = jnp.zeros((heads_local, HD), jnp.float32)
        qkv_shift = jnp.concatenate(
            [qv_shift[:, :HD], no_key_bias, qv_shift[:, HD:]], axis=1
        ).reshape(-1)
        packed = (
            jnp.dot(hidden_one_full, w_qkv, preferred_element_type=jnp.float32) + qkv_shift
        ).astype(jnp.bfloat16)
        packed_heads = to_heads(packed, heads_local)
        query_matrix = packed_heads[..., :HD]
        key_matrix_rows = packed_heads[..., HD : 2 * HD]
        value_rows = packed_heads[..., 2 * HD :]

        def head_forward(inputs):
            head_query_block, head_key_block, head_value_block = inputs
            scores = masked_scores(head_query_block, head_key_block, key_mask)
            row_peak = jnp.max(scores, -1, keepdims=True)
            row_exp = jnp.exp(scores - row_peak)
            row_sum = jnp.sum(row_exp, -1, keepdims=True)
            lowered_probabilities = (row_exp / row_sum).astype(jnp.bfloat16)
            context = jnp.einsum(
                "ycn,ynp->ycp",
                lowered_probabilities,
                head_value_block,
                preferred_element_type=jnp.float32,
            )
            return (context.astype(jnp.bfloat16), row_peak + jnp.log(row_sum))

        contexts, log_sums = lax.map(head_forward, (query_matrix, key_matrix_rows, value_rows))
        context = from_heads(contexts)
        attn_part = contract_last(context, w_out)
        attn_sum = lax.psum_scatter(attn_part, "tensor", scatter_dimension=1, tiled=True)
        middle = token_rows + attn_sum + out_shift
        normed_two, inverse_two = layer_stats(middle)
        hidden_two = (normed_two * gain_two + shift_two).astype(jnp.bfloat16)
        hidden_two_full = lax.all_gather(hidden_two, "tensor", axis=1, tiled=True)
        pre_act = jnp.dot(hidden_two_full, w_fc1, preferred_element_type=jnp.float32) + fc1_shift
        sig_act = jax.nn.sigmoid(1.702 * pre_act)
        active = (pre_act * sig_act).astype(jnp.bfloat16)
        mlp_part = contract_last(active, w_fc2)
        mlp_sum = lax.psum_scatter(
            mlp_part.astype(jnp.bfloat16), "tensor", scatter_dimension=1, tiled=True
        ).astype(jnp.float32)
        out_parts.append((middle + mlp_sum + fc2_shift).astype(jnp.bfloat16))
        weights_now = (
            lax.all_gather(qkv_weight, "dp", axis=0, tiled=True),
            lax.all_gather(out_weight, "dp", axis=0, tiled=True),
            lax.all_gather(fc1_weight, "dp", axis=0, tiled=True),
            lax.all_gather(fc2_weight, "dp", axis=0, tiled=True),
            lax.all_gather(qv_bias, "dp", axis=1, tiled=True),
            lax.all_gather(fc1_bias, "dp", axis=1, tiled=True),
            lax.all_gather(ln1_gain, "dp", axis=0, tiled=True),
            lax.all_gather(ln1_bias, "dp", axis=0, tiled=True),
            lax.all_gather(out_bias, "dp", axis=0, tiled=True),
            lax.all_gather(ln2_gain, "dp", axis=0, tiled=True),
            lax.all_gather(ln2_bias, "dp", axis=0, tiled=True),
            lax.all_gather(fc2_bias, "dp", axis=0, tiled=True),
        )
        w_qkv = weights_now[0]
        w_out = weights_now[1]
        w_fc1 = weights_now[2]
        w_fc2 = weights_now[3]
        gain_one = weights_now[6].astype(jnp.float32)
        gain_two = weights_now[9].astype(jnp.float32)
        cot_rows = cot_low.astype(jnp.float32)
        fc2_shift_grad = row_total(cot_rows)
        cot_full = lax.all_gather(cot_low, "tensor", axis=1, tiled=True)
        fc2_weight_grad = jnp.einsum(
            "bsd,bsf->df", cot_full, active, preferred_element_type=jnp.float32
        )
        act_grad = jnp.dot(cot_full, w_fc2, preferred_element_type=jnp.float32)
        pre_grad = act_grad * (sig_act + 1.702 * pre_act * sig_act * (1.0 - sig_act))
        fc1_shift_grad = row_total(pre_grad)
        pre_low = pre_grad.astype(jnp.bfloat16)
        fc1_weight_grad = jnp.einsum(
            "bsd,bsf->df", hidden_two_full, pre_low, preferred_element_type=jnp.float32
        )
        hidden_two_part = contract_last(pre_low, w_fc1)
        hidden_two_grad = lax.psum_scatter(
            hidden_two_part.astype(jnp.bfloat16), "tensor", scatter_dimension=1, tiled=True
        ).astype(jnp.float32)
        gain_two_grad = row_total(hidden_two_grad * normed_two)
        shift_two_grad = row_total(hidden_two_grad)
        middle_grad = cot_rows + stats_backward(hidden_two_grad, normed_two, inverse_two, gain_two)
        out_shift_grad = row_total(middle_grad)
        middle_low = middle_grad.astype(jnp.bfloat16)
        middle_full = lax.all_gather(middle_low, "tensor", axis=1, tiled=True)
        out_weight_grad = jnp.einsum(
            "bsd,bse->de", middle_full, context, preferred_element_type=jnp.float32
        )
        context_grad = jnp.dot(middle_full, w_out, preferred_element_type=jnp.float32).astype(
            jnp.bfloat16
        )

        def head_backward(inputs):
            head_query_block, head_key_block, head_value_block, per_head_gradient, head_lse = inputs
            scores = masked_scores(head_query_block, head_key_block, key_mask)
            probs = jnp.exp(scores - head_lse)
            probs_grad = jnp.einsum(
                "xjz,xez->xje",
                per_head_gradient,
                head_value_block,
                preferred_element_type=jnp.float32,
            )
            value_grad = jnp.einsum(
                "ozt,ozs->ots",
                probs.astype(jnp.bfloat16),
                per_head_gradient,
                preferred_element_type=jnp.float32,
            )
            inner = jnp.sum(probs_grad * probs, -1, keepdims=True)
            lowered_scores = (probs * (probs_grad - inner)).astype(jnp.bfloat16)
            query_grad = jnp.einsum(
                "ycn,ynp->ycp", lowered_scores, head_key_block, preferred_element_type=jnp.float32
            ) * HD ** (-0.5)
            key_grad = jnp.einsum(
                "ozt,ozs->ots", lowered_scores, head_query_block, preferred_element_type=jnp.float32
            ) * HD ** (-0.5)
            return (query_grad, key_grad, value_grad)

        query_grads, key_grads, value_grads = lax.map(
            head_backward,
            (
                query_matrix,
                key_matrix_rows,
                value_rows,
                to_heads(context_grad, heads_local),
                log_sums,
            ),
        )
        qv_shift_grad = jnp.concatenate(
            [jnp.sum(query_grads, axis=(1, 2)), jnp.sum(value_grads, axis=(1, 2))], axis=1
        )
        packed_low = from_heads(
            jnp.concatenate([query_grads, key_grads, value_grads], axis=-1)
        ).astype(jnp.bfloat16)
        qkv_weight_grad = jnp.einsum(
            "bsd,bsc->dc", hidden_one_full, packed_low, preferred_element_type=jnp.float32
        )
        hidden_one_part = contract_last(packed_low, w_qkv)
        hidden_one_grad = lax.psum_scatter(
            hidden_one_part.astype(jnp.bfloat16), "tensor", scatter_dimension=1, tiled=True
        ).astype(jnp.float32)
        gain_one_grad = row_total(hidden_one_grad * normed_one)
        shift_one_grad = row_total(hidden_one_grad)
        token_grad = middle_grad + stats_backward(
            hidden_one_grad, normed_one, inverse_one, gain_one
        )
        grad_parts.append(token_grad.astype(jnp.bfloat16))
        fresh = (
            qkv_weight_grad,
            out_weight_grad,
            fc1_weight_grad,
            fc2_weight_grad,
            qv_shift_grad,
            fc1_shift_grad.reshape(-1, 128),
            gain_one_grad,
            shift_one_grad,
            out_shift_grad,
            gain_two_grad,
            shift_two_grad,
            fc2_shift_grad,
        )
        totals = fresh if totals is None else jax.tree.map(jnp.add, totals, fresh)
    vector_sums = lax.psum(
        (totals[6], totals[7], totals[8], totals[9], totals[10], totals[11]), "tensor"
    )
    owned = (
        lax.psum_scatter(totals[0], "dp", scatter_dimension=0, tiled=True),
        lax.psum_scatter(totals[1], "dp", scatter_dimension=0, tiled=True),
        lax.psum_scatter(totals[2], "dp", scatter_dimension=0, tiled=True),
        lax.psum_scatter(totals[3], "dp", scatter_dimension=0, tiled=True),
        lax.psum_scatter(totals[4], "dp", scatter_dimension=1, tiled=True),
        lax.psum_scatter(totals[5], "dp", scatter_dimension=1, tiled=True),
        lax.psum_scatter(vector_sums[0], "dp", scatter_dimension=0, tiled=True),
        lax.psum_scatter(vector_sums[1], "dp", scatter_dimension=0, tiled=True),
        lax.psum_scatter(vector_sums[2], "dp", scatter_dimension=0, tiled=True),
        lax.psum_scatter(vector_sums[3], "dp", scatter_dimension=0, tiled=True),
        lax.psum_scatter(vector_sums[4], "dp", scatter_dimension=0, tiled=True),
        lax.psum_scatter(vector_sums[5], "dp", scatter_dimension=0, tiled=True),
    )
    return (
        jnp.concatenate(out_parts, axis=0),
        jnp.concatenate(grad_parts, axis=0),
        owned[6],
        owned[7],
        owned[0],
        owned[4],
        owned[1],
        owned[8],
        owned[9],
        owned[10],
        owned[2],
        owned[5],
        owned[3],
        owned[11],
    )


def solution(mesh):
    in_specs = (
        P("dp", "tensor", None),
        P("dp"),
        P("dp"),
        P("dp"),
        P("dp", "tensor"),
        P("tensor", "dp"),
        P("dp", "tensor"),
        P("dp"),
        P("dp"),
        P("dp"),
        P("dp", "tensor"),
        P("tensor", "dp"),
        P("dp", "tensor"),
        P("dp"),
        P("dp", "tensor", None),
    )
    out_specs = (
        P("dp", "tensor", None),
        P("dp", "tensor", None),
        P("dp"),
        P("dp"),
        P("dp", "tensor"),
        P("tensor", "dp"),
        P("dp", "tensor"),
        P("dp"),
        P("dp"),
        P("dp"),
        P("dp", "tensor"),
        P("tensor", "dp"),
        P("dp", "tensor"),
        P("dp"),
    )
    return jax.shard_map(body, mesh=mesh, in_specs=in_specs, out_specs=out_specs, check_vma=False)
```

profile of v0, /device:TPU:0, one launch (start us, length us, event | category | flops | bytes accessed | tf_op | source)
XLA Modules:
  0.0 1316.9 jit_solution(5674926109613073000)
XLA Ops:
  14.3 78.6 %all-reduce.31 = (bf16[1024]{0:T(1024)(128)(2,1)S(1)}, bf16[1024]{0:T(1024)(128)(2,1)S(1)}, bf16[1024]{0:T(1024)(128)(2,1)S(1)}, bf16[1024]{0:T(1024)(128)(2,1)S...) all-reduce(bf16[1024]{0:T(1024)(128)(2,1)S(1)} %dynamic-update-slic, ...), channel_id=1, replica_groups=mesh['dp'=16,'tensor'=2] {'dp'}, use_global_device_ids=true, to_apply=%add.1 | all-reduce | flops 6144 | bytes 24576
  114.1 35.9 %all_gather.88 = bf16[8,128]{0,1:T(8,128)(2,1)S(1)} all-gather(bf16[8,8]{0,1:T(8,128)(2,1)S(1)} %copy.128), channel_id=1, replica_groups=mesh['dp'=16,'tensor'=2] {'dp'}, dimensions={1}, use_global_device_ids=true | all-gather | bytes 2176 | tf_op jit(solution)/shard_map/all_gather | solution.py:81
  151.0 40.2 %all-gather.15.cloned.1.call-done = bf16[1024,1536]{1,0:T(8,128)(2,1)} async-done(((bf16[64,1536]{1,0:T(8,128)(2,1)}), bf16[1024,1536]{1,0:T(8,128)(2,1)}) %all-gather.15.cloned.1.call-update) | async-done | bytes 3145744 | tf_op jit(solution)/shard_map/all_gather | solution.py:77
  206.5 29.2 %while.56 = (s32[]{:T(128)}, bf16[8,1,580,64]{2,3,1,0:T(8,128)(2,1)S(1)}, f32[8,1,580,1]{2,3,1,0:T(1,128)S(1)}, bf16[8,1,580,64]{3,2,1,0:T(8,128)(2,1)S(1)}, bf1...) while((s32[]{:T(128)}, ...), condition=%wide.region_5.6_spmd.clone, body=%wide.region_2.5_spmd.clone.sunk | while | flops 88846720 | bytes 4749185 | solution.py:149
  235.8 11.9 all-gather.17.cloned.1.call-done
  274.3 29.6 %while.57 = (s32[]{:T(128)}, bf16[8,1,580,64]{2,3,1,0:T(8,128)(2,1)S(1)}, f32[8,1,580,1]{2,3,1,0:T(1,128)S(1)}, bf16[8,1,580,64]{3,2,1,0:T(8,128)(2,1)S(1)}, bf1...) while((s32[]{:T(128)}, ...), condition=%wide.region_15.16_spmd.clone, body=%wide.region_12.15_spmd.clone.sunk | while | flops 88846720 | bytes 4749185 | solution.py:149
  311.8 29.3 %all-reduce.36.cloned.1.call-done = (f32[1,580,1024]{2,0,1:T(1,128)}, f32[1,580,1024]{2,0,1:T(1,128)}) async-done(((f32[1,580,1024]{2,0,1:T(1,128)}, f32[1,580,1024]{2,0,1:T(1,128)}), (f32[1,580,1024]{2,0,1:T(1,128)}, f32[1,580,1024]{2,0,1:T(1,128)})) %all-reduce.36.cloned.1.call-update) | async-done | bytes 4751376
  365.4 42.0 %all_gather.95 = bf16[16,128]{0,1:T(8,128)(2,1)S(1)} all-gather(bf16[16,8]{0,1:T(8,128)(2,1)S(1)} %copy-done.43), channel_id=1, replica_groups=mesh['dp'=16,'tensor'=2] {'dp'}, dimensions={1}, use_global_device_ids=true | all-gather | bytes 4352 | tf_op jit(solution)/shard_map/all_gather | solution.py:82
  407.5 14.0 %all-gather.21.cloned.1.call-done = bf16[1024,2048]{1,0:T(8,128)(2,1)} async-done(((bf16[64,2048]{1,0:T(8,128)(2,1)}), bf16[1024,2048]{1,0:T(8,128)(2,1)}) %all-gather.21.cloned.1.call-update) | async-done | bytes 4194320 | tf_op jit(solution)/shard_map/all_gather | solution.py:79
  421.5 11.9 all-gather.19.cloned.1.call-done
  447.1 80.4 %all-gather.23.cloned.1.call-done = bf16[1024,2048]{1,0:T(8,128)(2,1)} async-done(((bf16[64,2048]{1,0:T(8,128)(2,1)}), bf16[1024,2048]{1,0:T(8,128)(2,1)}) %all-gather.23.cloned.1.call-update) | async-done | bytes 4194320 | tf_op jit(solution)/shard_map/all_gather | solution.py:80
  527.6 10.2 fusion.178
  592.0 10.5 multiply_reduce_fusion.3
  602.6 12.3 convert_reduce_fusion
  634.2 9.7 all-gather.35.cloned.1.call-done
  652.8 57.2 %while.58 = (s32[]{:T(128)}, f32[8,1,580,64]{2,3,1,0:T(8,128)S(1)}, bf16[8,1,580,64]{2,3,1,0:T(8,128)(2,1)}, f32[8,1,580,64]{2,3,1,0:T(8,128)S(1)}, bf16[8,1,580...) while((s32[]{:T(128)}, f32[8,1,580,64]{2,3,1,0:T(8,128)S(1)}, ...), condition=%wide.region_25.26_spmd.clone, body=%wide.region_23.25_spmd.clone.sunk | while | flops 218397840 | bytes 11886477 | solution.py:241
  716.3 70.0 %while.59 = (s32[]{:T(128)}, f32[8,1,580,64]{2,3,1,0:T(8,128)}, bf16[8,1,580,64]{2,3,1,0:T(8,128)(2,1)S(1)}, f32[8,1,580,64]{2,3,1,0:T(8,128)}, bf16[8,1,580,64]...) while((s32[]{:T(128)}, f32[8,1,580,64]{2,3,1,0:T(8,128)}, ...), condition=%wide.region_34.35_spmd.clone, body=%wide.region_32.34_spmd.clone.sunk | while | flops 218397840 | bytes 11587597 | solution.py:241
  826.9 9.4 copy.176
  864.1 8.9 fusion.158
  890.8 9.9 multiply_reduce_fusion.5
  900.7 82.6 %all-reduce.28 = (f32[1024]{0:T(1024)S(1)}, f32[1024]{0:T(1024)S(1)}, f32[8,128]{1,0:T(8,128)S(1)}, f32[1024]{0:T(1024)S(1)}, f32[1024]{0:T(1024)S(1)}, /*index=...) all-reduce(f32[1024]{0:T(1024)S(1)} %add.339, ...), channel_id=10, replica_groups=mesh['dp'=16,'tensor'=2] {'dp'}, use_global_device_ids=true, to_apply=%region_41.42.clone | all-reduce | flops 9216 | bytes 73728
  1000.6 9.0 add_convert_fusion.3
  1019.7 107.3 %reduce-scatter.31.cloned.1.call-done = f32[64,2048]{1,0:T(8,128)} async-done(((f32[1024,2048]{1,0:T(8,128)}), f32[64,2048]{1,0:T(8,128)}) %reduce-scatter.31.cloned.1.call-update) | async-done | bytes 524304 | tf_op jit(solution)/shard_map/reduce_scatter | solution.py:291
  1127.0 183.0 %reduce-scatter.33.cloned.1.call-done = f32[64,2048]{1,0:T(8,128)} async-done(((f32[1024,2048]{1,0:T(8,128)}), f32[64,2048]{1,0:T(8,128)}) %reduce-scatter.33.cloned.1.call-update) | async-done | bytes 524304
  (534 shorter events, 500.0 us)
Async XLA Ops:
  7.2 90.7 %copy-start = (bf16[2,290,1024]{2,0,1:T(2,128)(2,1)S(1)}, bf16[2,290,1024]{2,0,1:T(2,128)(2,1)}, u32[]{:S(2)}) copy-start(bf16[2,290,1024]{2,0,1:T(2,128)(2,1)} %param.23) | copy-start | bytes 3563524
  7.2 143.8 %all-gather.13.cloned.1.call-start = ((), (), s32[]{:S(2)}) async-start(), calls=%async_computation.4 | async-start | bytes 3563520 | tf_op jit(solution)/shard_map/all_gather | solution.py:121
  111.9 79.2 %all-gather.15.cloned.1.call-start = ((), (), s32[]{:S(2)}) async-start(), calls=%async_computation.5 | async-start | bytes 3342336 | tf_op jit(solution)/shard_map/all_gather | solution.py:77
  112.7 135.1 %all-gather.17.cloned.1.call-start = ((), (), s32[]{:S(2)}) async-start(), calls=%async_computation.6 | async-start | bytes 1114112 | tf_op jit(solution)/shard_map/all_gather | solution.py:78
  113.4 145.6 %all-gather.25.cloned.1.call-start = ((), (), s32[]{:S(2)}) async-start(), calls=%async_computation.10 | async-start | bytes 3563520 | tf_op jit(solution)/shard_map/all_gather | solution.py:121
  114.0 227.1 %all-reduce.36.cloned.1.call-start = ((), (), s32[]{:S(2)}) async-start(), calls=%async_computation.20 | async-start | bytes 9502720
  310.5 111.0 %all-gather.21.cloned.1.call-start = ((), (), s32[]{:S(2)}) async-start(), calls=%async_computation.8 | async-start | bytes 4456448 | tf_op jit(solution)/shard_map/all_gather | solution.py:79
  311.0 122.3 %all-gather.19.cloned.1.call-start = ((), (), s32[]{:S(2)}) async-start(), calls=%async_computation.7 | async-start | bytes 3563520 | tf_op jit(solution)/shard_map/all_gather | solution.py:156
  358.9 88.2 %all-gather.29.cloned.1.call-start = ((), (), s32[]{:S(2)}) async-start(), calls=%async_computation.12 | async-start | bytes 3563520 | tf_op jit(solution)/shard_map/all_gather | solution.py:187
  363.3 164.3 %all-gather.23.cloned.1.call-start = ((), (), s32[]{:S(2)}) async-start(), calls=%async_computation.9 | async-start | bytes 4456448 | tf_op jit(solution)/shard_map/all_gather | solution.py:80
  364.1 174.6 %all-gather.27.cloned.1.call-start = ((), (), s32[]{:S(2)}) async-start(), calls=%async_computation.11 | async-start | bytes 3563520 | tf_op jit(solution)/shard_map/all_gather | solution.py:156
  364.6 187.8 %all-gather.33.cloned.1.call-start = ((), (), s32[]{:S(2)}) async-start(), calls=%async_computation.14 | async-start | bytes 3563520 | tf_op jit(solution)/shard_map/all_gather | solution.py:187
  365.4 264.8 %all-gather.31.cloned.1.call-start = ((), (), s32[]{:S(2)}) async-start(), calls=%async_computation.13 | async-start | bytes 3563520 | tf_op jit(solution)/shard_map/all_gather | solution.py:207
  573.9 4.8 collective-permute-start.4
  577.4 8.3 collective-permute-start.2
  617.7 26.2 %all-gather.35.cloned.1.call-start = ((), (), s32[]{:S(2)}) async-start(), calls=%async_computation.15 | async-start | bytes 3563520 | tf_op jit(solution)/shard_map/all_gather | solution.py:207
  619.7 400.0 %reduce-scatter.29.cloned.1.call-start = ((), (), s32[]{:S(2)}) async-start(), calls=%async_computation.17 | async-start | bytes 2228224 | tf_op jit(solution)/shard_map/reduce_scatter | solution.py:290
  648.7 371.0 %reduce-scatter.27.cloned.1.call-start = ((), (), s32[]{:S(2)}) async-start(), calls=%async_computation.16 | async-start | bytes 6684672 | tf_op jit(solution)/shard_map/reduce_scatter | solution.py:289
  798.6 328.3 %reduce-scatter.31.cloned.1.call-start = ((), (), s32[]{:S(2)}) async-start(), calls=%async_computation.18 | async-start | bytes 8912896 | tf_op jit(solution)/shard_map/reduce_scatter | solution.py:291
  811.3 498.6 %reduce-scatter.33.cloned.1.call-start = ((), (), s32[]{:S(2)}) async-start(), calls=%async_computation.19 | async-start | bytes 8912896
  873.1 6.3 collective-permute-start.5
  875.4 8.5 collective-permute-start.3
  876.7 107.8 %collective-permute-start.1 = (bf16[6,1024]{1,0:T(8,128)(2,1)S(1)}, bf16[6,1024]{1,0:T(8,128)(2,1)S(1)}, u32[]{:S(2)}, u32[]{:S(2)}) collective-permute-start(bf16[6,1024]{1,0:T(8,128)(2,1)S(1)} %slice.67), channel_id=1, source_target_pairs={{0,1},{2,3},{4,5},{6,7},{8,9},{10,11},{12,13},{14,15},{16,17},{18,... | collective-permute-start | bytes 36872
  878.0 111.4 %collective-permute-start = (bf16[6,1024]{1,0:T(8,128)(2,1)S(1)}, bf16[6,1024]{1,0:T(8,128)(2,1)S(1)}, u32[]{:S(2)}, u32[]{:S(2)}) collective-permute-start(bf16[6,1024]{1,0:T(8,128)(2,1)S(1)} %slice.66), channel_id=1, source_target_pairs={{0,1},{2,3},{4,5},{6,7},{8,9},{10,11},{12,13},{14,15},{16,17},{18,... | collective-permute-start | bytes 36872
  (53 other events, 311.8 us)
Sparse Core Ops, SparseCore 0:
  112.0 6.8 all-gather.12
  121.7 69.3 all-gather.14
  193.9 53.8 all-gather.16
  249.1 9.7 all-gather.24
  310.6 30.4 all-reduce.35
  344.0 77.3 all-gather.20
  423.7 9.6 all-gather.18
  434.9 12.1 all-gather.28
  450.3 77.2 all-gather.22
  529.0 9.5 all-gather.26
  540.3 12.1 all-gather.32
  617.9 12.2 all-gather.30
  631.8 12.1 all-gather.34
  648.8 82.0 reduce-scatter.28
  798.7 148.0 reduce-scatter.26
  949.7 177.2 reduce-scatter.30
  1129.8 180.1 reduce-scatter.32
where the time goes:
time: 1330 us; the launch traced here: 1320 us
  waiting for transfers between devices  515 us (39%)
  matrix products  287 us (22%)
  blocking collectives  258 us (19%)
  other arithmetic  126 us (9%)
  local copies, waits for them, and re-layouts  100 us (8%)
  between operations  18.7 us (1%)
    unnamed x25, waiting for transfers between devices  217 us
    unnamed x4, blocking collectives  177 us
    reduce_scatter x1, waiting for transfers between devices, body(): lax.psum_scatter(totals[2], 'dp', scatter_dimension=0, tiled=True)  107 us
    all_gather x1, waiting for transfers between devices, body(): lax.all_gather(fc2_weight, 'dp', axis=0, tiled=True)  80.4 us
    unnamed x157, local copies, waits for them, and re-layouts  75.6 us
    dot_general x32, matrix products, masked_scores(): jnp.einsum('xjz,xez->xje', query_matrix, key_matrix_rows, preferred_eleme...  45.4 us
    all_gather x1, blocking collectives, body(): lax.all_gather(fc1_bias, 'dp', axis=1, tiled=True)  42 us
    all_gather x1, waiting for transfers between devices, body(): lax.all_gather(qkv_weight, 'dp', axis=0, tiled=True)  40.2 us
  transfers between devices with their start and end apart: 23, of which 14 were waited for; matrix products, arithmetic and copies ran while one was open for 30% of the time, Pallas kernels for 0%

commit v1 on v0

v1 whole, which is shorter than its diff:
```python
import functools

import jax
import jax.numpy as jnp
from jax import lax
from jax.experimental import pallas as pl
from jax.experimental.pallas import tpu as pltpu
from jax.sharding import PartitionSpec as P

HD = 64
UNIT = 256
SLAB = 128
RING = 4
BLOCKS = (4, 2, 2)
VEC_ROWS = 48
GVEC_ROWS = 40
F32 = jnp.float32
BF16 = jnp.bfloat16
MESH = pl.DeviceIdType.MESH


def mm(left, right, left_dim, right_dim):
    return lax.dot_general(
        left, right, (((left_dim,), (right_dim,)), ((), ())), preferred_element_type=F32
    )


def when(condition, action):
    if isinstance(condition, bool):
        if condition:
            action()
    else:
        pl.when(condition)(action)


def stats(values):
    center = values - jnp.mean(values, -1, keepdims=True)
    inverse = lax.rsqrt(jnp.mean(center * center, -1, keepdims=True) + 1e-05)
    return center * inverse, inverse


def stats_back(scaled, normed, inverse):
    return inverse * (
        scaled
        - jnp.mean(scaled, -1, keepdims=True)
        - normed * jnp.mean(scaled * normed, -1, keepdims=True)
    )


def three_terms(values):
    first = values.astype(BF16).astype(F32)
    second = (values - first).astype(BF16).astype(F32)
    return first, second, values - first - second


def layer_kernel(
    images,
    half,
    rows_half,
    linked,
    lengths,
    tok,
    cot_in,
    vec_in,
    wq_in,
    wo_in,
    w1_in,
    w2_in,
    result,
    tok_grad,
    gq,
    go,
    g1,
    g2,
    gvec,
    buf,
    h1,
    qkv,
    ctx,
    h2,
    act,
    gp,
    cot,
    mid,
    own,
    snd,
    rcv,
    lse,
    vec,
    acc,
    r1,
    r2,
    r3,
    vb,
    vbr,
    vs,
    vr,
    local_sem,
    cot_sem,
    gs,
    gr,
    hs,
    hr,
    xs,
    xr,
    ts,
    tr,
    vgs,
    vgr,
    vss,
    vsr,
):
    R = rows_half
    T = images * 2 * R
    D = tok.shape[-1]
    d_idx = lax.axis_index("dp")
    t_idx = lax.axis_index("tensor")
    core = {"dp": d_idx, "tensor": 1 - t_idx}
    if linked:
        x = lax.rem(d_idx, 2)
        y = lax.rem(lax.div(d_idx, 2), 2)
        z = lax.div(d_idx, 4)

        def chip(zz, yy, xx):
            return {"dp": (zz * 2 + yy) * 2 + xx, "tensor": t_idx}

        xdev = chip(z, y, 1 - x)
        ydev = chip(z, 1 - y, x)
        zdev = [chip(lax.rem(z + k, 4), y, x) for k in (1, 2, 3)]
    else:
        x = y = z = 0
        xdev = ydev = None
        zdev = []

    def remote(src, dst, send, recv, device):
        return pltpu.make_async_remote_copy(
            src_ref=src,
            dst_ref=dst,
            send_sem=send,
            recv_sem=recv,
            device_id=device,
            device_id_type=MESH,
        )

    def start(copies):
        for copy in copies:
            copy.start()

    def wait(copies):
        for copy in copies:
            copy.wait()

    barrier = pltpu.get_barrier_semaphore()
    peers = [core] + ([xdev, ydev] + zdev if linked else [])
    for peer in peers:
        pl.semaphore_signal(barrier, inc=1, device_id=peer, device_id_type=MESH)

    def unit_source(s):
        ref, u = (
            (wq_in, s)
            if s < 6
            else (wo_in, s - 6)
            if s < 8
            else (w1_in, s - 8)
            if s < 16
            else (w2_in, s - 16)
        )
        cols = pl.ds(u * UNIT, UNIT)
        return ref.at[:, cols] if linked else ref.at[:, :, :, :, cols]

    def place(s):
        return s + 16 - 16 * (s // 8)

    def place_dyn(s):
        return s + 16 - 16 * lax.div(s, 8)

    weight_copies = []
    for s in range(24):
        target = buf.at[place(s), z, y, x] if linked else buf.at[place(s)]
        weight_copies.append(pltpu.make_async_copy(unit_source(s), target, local_sem.at[s]))
    start(weight_copies)
    cot_copies = [
        pltpu.make_async_copy(cot_in.at[i], cot.at[pl.ds(i * 2 * R, R)], cot_sem.at[i])
        for i in range(images)
    ]
    start(cot_copies)
    pl.semaphore_wait(barrier, len(peers))

    def spread1(s):
        u, slot = place_dyn(s), lax.rem(s, RING)
        block = buf.at[u, z, y, x]
        return [
            remote(block, block, gs.at[slot, k], gr.at[slot, k], zdev[k]) for k in range(3)
        ]

    def spread2(s):
        u, slot = place_dyn(s), lax.rem(s, RING)
        a = buf.at[u, :, y, x, pl.ds(0, 32)]
        b = buf.at[u, :, y, x, pl.ds(32, 32)]
        return [
            remote(a, a, gs.at[slot, 3], gr.at[slot, 3], xdev),
            remote(b, b, gs.at[slot, 4], gr.at[slot, 4], ydev),
        ]

    def spread3(s):
        u, slot = place_dyn(s), lax.rem(s, RING)
        a = buf.at[u, :, y, :, pl.ds(0, 32)]
        b = buf.at[u, :, :, x, pl.ds(32, 32)]
        return [
            remote(a, a, gs.at[slot, 5], gr.at[slot, 5], ydev),
            remote(b, b, gs.at[slot, 6], gr.at[slot, 6], xdev),
        ]

    def gather_tick(s):
        if not linked:
            return
        s = jnp.int32(s)

        def begin():
            start(spread1(s))

        def second():
            wait(spread1(s - 1))
            start(spread2(s - 1))

        def third():
            wait(spread2(s - 2))
            start(spread3(s - 2))

        def end():
            wait(spread3(s - 3))

        when(s < 24, begin)
        when((s >= 1) & (s < 25), second)
        when((s >= 2) & (s < 26), third)
        when((s >= 3) & (s < 27), end)

    def grad_place(r):
        return lax.rem(r + 24, 32)

    def first(r):
        g, slot = grad_place(r), lax.rem(r, RING)
        return [
            remote(
                buf.at[g, :, 1 - y, :, pl.ds(0, 32)],
                r1.at[slot, 0],
                hs.at[slot, 0],
                hr.at[slot, 0],
                ydev,
            ),
            remote(
                buf.at[g, :, :, 1 - x, pl.ds(32, 32)],
                r1.at[slot, 1],
                hs.at[slot, 1],
                hr.at[slot, 1],
                xdev,
            ),
        ]

    def second_step(r):
        g, slot = grad_place(r), lax.rem(r, RING)
        return [
            remote(
                buf.at[g, :, y, 1 - x, pl.ds(0, 32)],
                r2.at[slot, 0],
                hs.at[slot, 2],
                hr.at[slot, 2],
                xdev,
            ),
            remote(
                buf.at[g, :, 1 - y, x, pl.ds(32, 32)],
                r2.at[slot, 1],
                hs.at[slot, 3],
                hr.at[slot, 3],
                ydev,
            ),
        ]

    def third_step(r):
        g, slot = grad_place(r), lax.rem(r, RING)
        return [
            remote(
                buf.at[g, lax.rem(z + k + 1, 4), y, x],
                r3.at[slot, k],
                hs.at[slot, 4 + k],
                hr.at[slot, 4 + k],
                zdev[k],
            )
            for k in range(3)
        ]

    def add1(r):
        g, slot = grad_place(r), lax.rem(r, RING)
        top = buf[g, :, y, :, pl.ds(0, 32)].astype(F32) + r1[slot, 0].astype(F32)
        buf[g, :, y, :, pl.ds(0, 32)] = top.astype(BF16)
        low = buf[g, :, :, x, pl.ds(32, 32)].astype(F32) + r1[slot, 1].astype(F32)
        buf[g, :, :, x, pl.ds(32, 32)] = low.astype(BF16)

    def add2(r):
        g, slot = grad_place(r), lax.rem(r, RING)
        top = buf[g, :, y, x, pl.ds(0, 32)].astype(F32) + r2[slot, 0].astype(F32)
        buf[g, :, y, x, pl.ds(0, 32)] = top.astype(BF16)
        low = buf[g, :, y, x, pl.ds(32, 32)].astype(F32) + r2[slot, 1].astype(F32)
        buf[g, :, y, x, pl.ds(32, 32)] = low.astype(BF16)

    def add3(r):
        g, slot = grad_place(r), lax.rem(r, RING)
        total = buf[g, z, y, x].astype(F32)
        for k in range(3):
            total = total + r3[slot, k].astype(F32)

        def put(ref, base):
            def store():
                ref[:, pl.ds(pl.multiple_of((r - base) * UNIT, UNIT), UNIT)] = total

            return store

        when(r < 8, put(g2, 0))
        when((r >= 8) & (r < 16), put(g1, 8))
        when((r >= 16) & (r < 18), put(go, 16))
        when(r >= 18, put(gq, 18))

    def scatter_tick(s):
        if not linked:
            return
        s = jnp.int32(s)

        def begin():
            start(first(s))

        def second():
            wait(first(s - 1))
            add1(s - 1)
            start(second_step(s - 1))

        def third():
            wait(second_step(s - 2))
            add2(s - 2)
            start(third_step(s - 2))

        def end():
            wait(third_step(s - 3))
            add3(s - 3)

        when((s >= 0) & (s < 24), begin)
        when((s >= 1) & (s < 25), second)
        when((s >= 2) & (s < 26), third)
        when((s >= 3) & (s < 27), end)

    def put_grad(r, value):
        buf[grad_place(r)] = value.astype(BF16).reshape(BLOCKS + (D // 16, UNIT))
        if not linked:

            def put(ref, base):
                def store():
                    cols = pl.ds(pl.multiple_of((r - base) * UNIT, UNIT), UNIT)
                    copy = pltpu.make_async_copy(
                        buf.at[grad_place(r)], ref.at[:, :, :, :, cols], local_sem.at[0]
                    )
                    copy.start()
                    copy.wait()

                return store

            when(r < 8, put(g2, 0))
            when((r >= 8) & (r < 16), put(g1, 8))
            when((r >= 16) & (r < 18), put(go, 16))
            when(r >= 18, put(gq, 18))

    def weight(place_idx):
        return buf[place_idx].reshape(D, UNIT)

    def pair(ref, n):
        return jnp.concatenate([ref[2 * n], ref[2 * n + 1]], axis=1)

    def put_pair(ref, n, value):
        ref[2 * n] = value[:, :SLAB]
        ref[2 * n + 1] = value[:, SLAB:]

    def token_exchange(which, ref, i):
        return remote(
            ref.at[pl.ds(i * 2 * R, R)],
            ref.at[pl.ds((i * 2 + 1) * R, R)],
            ts.at[which, i],
            tr.at[which, i],
            core,
        )

    def partial_exchange(which, side, j):
        return remote(snd.at[j], rcv.at[side, j], xs.at[which, j], xr.at[which, j], core)

    def project(which, side, slabs, places, tick=None):
        groups = len(places)

        def one(j, carry):
            left = jnp.concatenate([ref[n] for ref, n in slabs], axis=1)
            right = jnp.concatenate(
                [buf[u, j].reshape(UNIT, UNIT) for u in places], axis=1
            )
            total = mm(left, right, 1, 1)
            for i in range(images):
                own[j, pl.ds(i * R, R)] = total[i * 2 * R : (i * 2 + 1) * R]
                snd[j, pl.ds(i * R, R)] = total[(i * 2 + 1) * R : (i * 2 + 2) * R].astype(BF16)
            partial_exchange(which, side, j).start()
            if tick is not None:
                tick(j)
            return carry

        del groups
        lax.fori_loop(0, D // UNIT, one, 0)

    def partial_wait(which, side):
        for j in range(D // UNIT):
            partial_exchange(which, side, j).wait()

    def summed(side, rows):
        return jnp.concatenate(
            [own[j, rows] + rcv[side, j, rows].astype(F32) for j in range(D // UNIT)], axis=1
        )

    CHUNK = 16

    def token_loop(i, body):
        def step(c, carry):
            r = pl.multiple_of(i * R + c * CHUNK, CHUNK)
            full = pl.multiple_of(i * 2 * R + c * CHUNK, CHUNK)
            body(pl.ds(r, CHUNK), pl.ds(full, CHUNK))
            return carry

        lax.fori_loop(0, R // CHUNK, step, 0, unroll=1)

    def tokens_of(i, rows):
        return tok[rows].astype(F32)

    if linked:
        vb[0] = vec_in[...]

        def vec_copy(k, stage, device):
            return remote(vb.at[stage], vbr.at[k], vgs.at[k], vgr.at[k], device)

        vx = vec_copy(0, 0, xdev)
        vx.start()
        wait(weight_copies[:6])
        gather_tick(0)
        vx.wait()
        vb[1] = vb[0] + vbr[0]
        vy = vec_copy(1, 1, ydev)
        vy.start()
        gather_tick(1)
        vy.wait()
        vb[2] = vb[1] + vbr[1]
        vz = [vec_copy(2 + k, 2, zdev[k]) for k in range(3)]
        start(vz)
        gather_tick(2)
        wait(vz)
        vec[...] = (
            vb[2].astype(F32) + vbr[2].astype(F32) + vbr[3].astype(F32) + vbr[4].astype(F32)
        )
    else:
        wait(weight_copies[:6])
        vec[...] = vec_in[...].astype(F32)

    def vector(n):
        return jnp.concatenate([vec[4 * n + k : 4 * n + k + 1] for k in range(4)], axis=1)

    gain1, shift1, out_bias, gain2, shift2, fc2_bias = [vector(n) for n in range(6)]
    gvec[...] = jnp.zeros_like(gvec)
    acc[...] = jnp.zeros_like(acc)
    lse[...] = jnp.zeros_like(lse)

    for i in range(images):

        def norm_one(rows, full):
            normed, _ = stats(tok[rows].astype(F32))
            h1[full] = (normed * gain1 + shift1).astype(BF16)

        token_loop(i, norm_one)
        token_exchange(0, h1, i).start()
    wait(weight_copies[6:])
    wait(cot_copies)
    for i in range(images):
        token_exchange(1, cot, i).start()
    for s in (3, 4, 5):
        gather_tick(s)
    for i in range(images):
        token_exchange(0, h1, i).wait()
        token_exchange(1, cot, i).wait()

    lane = lax.broadcasted_iota(jnp.int32, (2 * R, SLAB), 1)
    row = lax.broadcasted_iota(jnp.int32, (2 * R, SLAB), 0)
    second_half = row >= R
    inside = jnp.where(second_half, row - R, row)
    position = inside + jnp.where(second_half, (1 - t_idx) * half, t_idx * half)
    low_lanes = lane[:R] < HD

    def head_lanes(e, lanes):
        return lanes < HD if e == 0 else lanes >= HD

    def extra(e):
        return HD * (1 - e)

    def key_bias(i):
        valid = (inside < half) & (position < lengths[i])
        return jnp.where(valid, 0.0, -1e30)

    def project_heads(c):
        def one(j, carry):
            u = 3 * c + j
            value = mm(h1[...], weight(16 + u), 1, 0) + vec[pl.ds(24 + u, 1)]
            put_pair(qkv, u, value.astype(BF16))
            return carry

        lax.fori_loop(0, 3, one, 0)

    def attend(i, c, p):
        rows = pl.ds(pl.multiple_of(i * 2 * R, 16), 2 * R)
        q = qkv[c * 6 + p, rows].astype(F32) * HD**-0.5
        k = qkv[c * 6 + 2 + p, rows].astype(F32)
        v = qkv[c * 6 + 4 + p, rows]
        bias = key_bias(i)
        heads = []
        for e in range(2):
            inhead = head_lanes(e, lane)
            first_extra = lane == extra(e)
            qm = jnp.where(inhead, q, jnp.where(first_extra, 1.0, 0.0)).astype(BF16)
            km = jnp.where(inhead, k, jnp.where(first_extra, bias, 0.0)).astype(BF16)
            heads.append((qm, km))
        for m in range(2):
            outs, sums = [], []
            for e in range(2):
                qm, km = heads[e]
                scores = mm(qm[m * R : (m + 1) * R], km, 1, 1)
                peak = jnp.max(scores, -1, keepdims=True)
                exps = jnp.exp(scores - peak)
                total = jnp.sum(exps, -1, keepdims=True)
                outs.append(mm(exps.astype(BF16), v, 1, 0) * (1.0 / total))
                sums.append(peak + jnp.log(total))
            tile = pl.ds(pl.multiple_of(i * 2 * R + m * R, 16), R)
            ctx[2 * c + p, tile] = jnp.where(low_lanes, outs[0], outs[1]).astype(BF16)
            column = lane[:R]
            head = (2 * c + p) * 2
            lse[tile] = jnp.where(
                column == head, sums[0], jnp.where(column == head + 1, sums[1], lse[tile])
            )

    for c in range(2):
        project_heads(c)

        def attend_step(n, carry):
            gather_tick(6 + 4 * c + n)
            attend(lax.div(n, 2), c, lax.rem(n, 2))
            return carry

        lax.fori_loop(0, images * 2, attend_step, 0)

    project(0, 0, [(ctx, n) for n in range(4)], [22, 23])
    gather_tick(14)
    partial_wait(0, 0)
    for i in range(images):

        def norm_two(rows, full):
            middle = tok[rows].astype(F32) + summed(0, rows) + out_bias
            mid[rows] = middle
            normed, _ = stats(middle)
            h2[full] = (normed * gain2 + shift2).astype(BF16)

        token_loop(i, norm_two)
        token_exchange(2, h2, i).start()
        if i == 0:
            gather_tick(15)
    for i in range(images):
        token_exchange(2, h2, i).wait()

    def hidden(u, carry):
        if linked:
            pl.when(lax.rem(u, 2) == 0)(lambda: gather_tick(16 + lax.div(u, 2)))
        pre = mm(h2[...], weight(8 + u), 1, 0) + vec[pl.ds(30 + u, 1)]
        sig = 0.5 * jnp.tanh(0.851 * pre) + 0.5
        active = pre * sig
        slope = sig + 1.702 * active * (1.0 - sig)
        put_pair(act, u, active.astype(BF16))
        put_pair(gp, u, slope.astype(BF16))
        return carry

    lax.fori_loop(0, 8, hidden, 0)

    def hidden_back(u, carry):
        put_grad(u, mm(cot[...], pair(act, u), 0, 0))
        gather_tick(20 + u)
        pre_grad = mm(cot[...], weight(u), 1, 0) * pair(gp, u).astype(F32)
        gvec[pl.ds(28 + u, 1)] = jnp.sum(pre_grad, 0, keepdims=True)
        put_pair(gp, u, pre_grad.astype(BF16))
        scatter_tick(u - 2)
        return carry

    lax.fori_loop(0, 8, hidden_back, 0)

    def odd_tick(base):
        if not linked:
            return None

        def tick(j):
            pl.when(lax.rem(j, 2) == 1)(lambda: scatter_tick(base + lax.div(j, 2)))

        return tick

    project(1, 1, [(act, n) for n in range(16)], list(range(8)), odd_tick(6))

    def first_grad(u, carry):
        put_grad(8 + u, mm(h2[...], pair(gp, u), 0, 0))
        if linked:
            pl.when(lax.rem(u, 3) == 2)(lambda: scatter_tick(8 + lax.div(u, 3)))
        return carry

    lax.fori_loop(0, 8, first_grad, 0)
    scatter_tick(10)
    partial_wait(1, 1)
    for i in range(images):

        def finish(rows, full):
            total = mid[rows] + summed(1, rows) + fc2_bias
            result[rows] = total.astype(BF16)

        token_loop(i, finish)
    project(2, 0, [(gp, n) for n in range(16)], list(range(8, 16)), odd_tick(11))
    partial_wait(2, 0)

    def add_rows(n, value):
        acc[n] += value[:8] + value[8:]

    for i in range(images):

        def norm_two_back(rows, full):
            grad = summed(0, rows)
            normed, inverse = stats(mid[rows])
            cots = cot[full].astype(F32)
            middle_grad = cots + stats_back(grad * gain2, normed, inverse)
            add_rows(2, middle_grad)
            add_rows(3, grad * normed)
            add_rows(4, grad)
            add_rows(5, cots)
            mid[rows] = middle_grad
            cot[full] = middle_grad.astype(BF16)

        token_loop(i, norm_two_back)
        token_exchange(3, cot, i).start()
        if i == 0:
            scatter_tick(13)
    for i in range(images):
        token_exchange(3, cot, i).wait()

    def out_back(u, carry):
        put_grad(16 + u, mm(cot[...], pair(ctx, u), 0, 0))
        value = mm(cot[...], weight(22 + u), 1, 0)
        put_pair(act, 6 + u, value.astype(BF16))
        return carry

    lax.fori_loop(0, 2, out_back, 0)
    scatter_tick(14)

    def attend_back(i, c, p):
        rows = pl.ds(pl.multiple_of(i * 2 * R, 16), 2 * R)
        q = qkv[c * 6 + p, rows].astype(F32) * HD**-0.5
        k = qkv[c * 6 + 2 + p, rows]
        v = qkv[c * 6 + 4 + p, rows]
        up = act[12 + 2 * c + p, rows]
        inner_all = up.astype(F32) * ctx[2 * c + p, rows].astype(F32)
        sums_all = lse[rows]
        bias = key_bias(i)
        q_low = q.astype(BF16)
        q_grads, k_grads, v_grads = [], [], []
        for e in range(2):
            inhead = head_lanes(e, lane)
            at = [lane == extra(e) + n for n in range(4)]
            head = (2 * c + p) * 2 + e
            total = jnp.sum(jnp.where(lane == head, sums_all, 0.0), -1, keepdims=True)
            inner = jnp.sum(jnp.where(inhead, inner_all, 0.0), -1, keepdims=True)
            s1, s2, s3 = three_terms(-total)
            n1, n2, n3 = three_terms(-inner)
            ones = at[1] | at[2] | at[3]
            qa = jnp.where(
                inhead,
                q,
                jnp.where(
                    at[0],
                    1.0,
                    jnp.where(at[1], s1, jnp.where(at[2], s2, jnp.where(at[3], s3, 0.0))),
                ),
            ).astype(BF16)
            ka = jnp.where(
                inhead, k.astype(F32), jnp.where(at[0], bias, jnp.where(ones, 1.0, 0.0))
            ).astype(BF16)
            ua = jnp.where(
                inhead,
                up.astype(F32),
                jnp.where(at[1], n1, jnp.where(at[2], n2, jnp.where(at[3], n3, 0.0))),
            ).astype(BF16)
            va = jnp.where(inhead, v.astype(F32), jnp.where(ones, 1.0, 0.0)).astype(BF16)
            q_grad = None
            k_parts, v_parts = [], []
            for m in range(2):
                tile = slice(m * R, (m + 1) * R)
                probs = jnp.exp(mm(ka[tile], qa, 1, 1))
                grads = (probs * mm(va[tile], ua, 1, 1)).astype(BF16)
                v_parts.append(mm(probs.astype(BF16), up, 1, 0))
                k_parts.append(mm(grads, q_low, 1, 0))
                part = mm(grads, k[tile], 0, 0)
                q_grad = part if q_grad is None else q_grad + part
            q_grads.append(q_grad * HD**-0.5)
            k_grads.append(k_parts)
            v_grads.append(v_parts)
        low = lane < HD
        q_sum = jnp.where(low, q_grads[0], q_grads[1])
        act[c * 6 + p, rows] = q_sum.astype(BF16)
        v_bias = None
        for m in range(2):
            tile = pl.ds(pl.multiple_of(i * 2 * R + m * R, 16), R)
            k_sum = jnp.where(low_lanes, k_grads[0][m], k_grads[1][m])
            v_sum = jnp.where(low_lanes, v_grads[0][m], v_grads[1][m])
            act[c * 6 + 2 + p, tile] = k_sum.astype(BF16)
            act[c * 6 + 4 + p, tile] = v_sum.astype(BF16)
            part = jnp.sum(v_sum, 0, keepdims=True)
            v_bias = part if v_bias is None else v_bias + part
        bias_row = jnp.concatenate([jnp.sum(q_sum, 0, keepdims=True), v_bias], axis=1)
        gvec[pl.ds(24 + 2 * c + p, 1)] += bias_row

    for c in range(2):

        def attend_back_step(n, carry):
            if linked:
                pl.when(n < 3)(lambda: scatter_tick(15 + 3 * c + n))
            attend_back(lax.div(n, 2), c, lax.rem(n, 2))
            return carry

        lax.fori_loop(0, images * 2, attend_back_step, 0)

        def heads_grad(j, carry):
            u = 3 * c + j
            put_grad(18 + u, mm(h1[...], pair(act, u), 0, 0))
            return carry

        lax.fori_loop(0, 3, heads_grad, 0)
    scatter_tick(21)
    project(3, 1, [(act, n) for n in range(12)], list(range(16, 22)), odd_tick(22))
    partial_wait(3, 1)
    for i in range(images):

        def norm_one_back(rows, full):
            grad = summed(1, rows)
            normed, inverse = stats(tok[rows].astype(F32))
            add_rows(0, grad * normed)
            add_rows(1, grad)
            total = mid[rows] + stats_back(grad * gain1, normed, inverse)
            tok_grad[rows] = total.astype(BF16)

        token_loop(i, norm_one_back)
        if i == 0:
            scatter_tick(24)

    for n in range(6):
        total = jnp.sum(acc[n], 0, keepdims=True)
        for k in range(4):
            gvec[4 * n + k : 4 * n + k + 1] = total[:, k * UNIT : (k + 1) * UNIT]

    def sum_copy(k, stage, device):
        return remote(vs.at[stage], vr.at[k], vss.at[k], vsr.at[k], device)

    vs[0] = gvec[...]
    over_core = sum_copy(0, 0, core)
    over_core.start()
    scatter_tick(25)
    over_core.wait()
    shared = lax.broadcasted_iota(jnp.int32, (GVEC_ROWS, UNIT), 0) < 24
    gathered = vs[0] + jnp.where(shared, vr[0], 0.0)
    if linked:
        vs[1] = gathered
        over_x = sum_copy(1, 1, xdev)
        over_x.start()
        scatter_tick(26)
        over_x.wait()
        vs[2] = vs[1] + vr[1]
        over_y = sum_copy(2, 2, ydev)
        over_y.start()
        over_y.wait()
        vs[3] = vs[2] + vr[2]
        over_z = [sum_copy(3 + k, 3, zdev[k]) for k in range(3)]
        start(over_z)
        wait(over_z)
        gvec[...] = vs[3] + vr[3] + vr[4] + vr[5]
    else:
        gvec[...] = gathered


def own_part(values, index, width):
    return lax.dynamic_slice_in_dim(values, index * width, width, axis=1)


def body(
    linked,
    tokens,
    lengths,
    ln1_gain,
    ln1_bias,
    qkv_weight,
    qv_bias,
    out_weight,
    out_bias,
    ln2_gain,
    ln2_bias,
    fc1_weight,
    fc1_bias,
    fc2_weight,
    fc2_bias,
    cotangent,
):
    images, half, D = tokens.shape
    parts = lax.axis_size("dp")
    dp = lax.axis_index("dp")
    heads = qv_bias.shape[0]
    R = -(-half // 16) * 16
    T = images * 2 * R
    share = D // parts
    pad = ((0, 0), (0, R - half), (0, 0))
    tok = jnp.pad(tokens, pad).reshape(images * R, D)
    cot = jnp.pad(cotangent, pad)

    def placed(values, width):
        if linked:
            wide = jnp.tile(values, (1, parts))
            at = lax.broadcasted_iota(jnp.int32, wide.shape, 1) // width == dp
            return jnp.where(at, wide, jnp.zeros_like(wide))
        return lax.all_gather(values, "dp", axis=1, tiled=True)

    norms = placed(
        jnp.stack([ln1_gain, ln1_bias, out_bias, ln2_gain, ln2_bias, fc2_bias]), share
    ).reshape(24, UNIT)
    qv = placed(qv_bias, 2 * HD // parts if linked else 1).reshape(2, 2, 2, 2, HD)
    q_rows = qv[:, :, :, 0].reshape(2, 1, UNIT)
    v_rows = qv[:, :, :, 1].reshape(2, 1, UNIT)
    qkv_rows = jnp.concatenate([q_rows, jnp.zeros_like(q_rows), v_rows], axis=1).reshape(6, UNIT)
    fc1_rows = placed(fc1_bias, 128 // parts if linked else 1).reshape(8, UNIT)
    vec = jnp.concatenate(
        [norms, qkv_rows, fc1_rows, jnp.zeros((VEC_ROWS - 38, UNIT), BF16)], axis=0
    )

    grouped = qkv_weight.reshape(share, heads // 4, 4, 3, HD)
    wq = jnp.swapaxes(grouped, 2, 3).reshape(share, heads * 3 * HD)
    weights = [wq, out_weight, fc1_weight, fc2_weight]
    if not linked:
        weights = [
            lax.all_gather(w, "dp", axis=0, tiled=True).reshape(
                BLOCKS + (D // 16, w.shape[1])
            )
            for w in weights
        ]
    vmem = pl.BlockSpec(memory_space=pltpu.VMEM)
    hbm = pl.BlockSpec(memory_space=pl.ANY)
    if linked:
        grads = [jax.ShapeDtypeStruct(w.shape, F32) for w in weights]
    else:
        grads = [jax.ShapeDtypeStruct(w.shape, BF16) for w in weights]
    grad_spec = vmem if linked else hbm
    dma = pltpu.SemaphoreType.DMA
    block = BLOCKS + (D // 16, UNIT)
    outs = pl.pallas_call(
        functools.partial(layer_kernel, images, half, R, linked),
        out_shape=[
            jax.ShapeDtypeStruct((images * R, D), BF16),
            jax.ShapeDtypeStruct((images * R, D), BF16),
            *grads,
            jax.ShapeDtypeStruct((GVEC_ROWS, UNIT), F32),
        ],
        in_specs=[pl.BlockSpec(memory_space=pltpu.SMEM), vmem, hbm, vmem, hbm, hbm, hbm, hbm],
        out_specs=[vmem, vmem, grad_spec, grad_spec, grad_spec, grad_spec, vmem],
        scratch_shapes=[
            pltpu.VMEM((32,) + block, BF16),
            pltpu.VMEM((T, D), BF16),
            pltpu.VMEM((12, T, SLAB), BF16),
            pltpu.VMEM((4, T, SLAB), BF16),
            pltpu.VMEM((T, D), BF16),
            pltpu.VMEM((16, T, SLAB), BF16),
            pltpu.VMEM((16, T, SLAB), BF16),
            pltpu.VMEM((T, D), BF16),
            pltpu.VMEM((images * R, D), F32),
            pltpu.VMEM((4, images * R, UNIT), F32),
            pltpu.VMEM((4, images * R, UNIT), BF16),
            pltpu.VMEM((2, 4, images * R, UNIT), BF16),
            pltpu.VMEM((T, SLAB), F32),
            pltpu.VMEM((VEC_ROWS, UNIT), F32),
            pltpu.VMEM((6, 8, D), F32),
            pltpu.VMEM((RING, 2, 4, 2, 32, UNIT), BF16),
            pltpu.VMEM((RING, 2, 4, 32, UNIT), BF16),
            pltpu.VMEM((RING, 3, 64, UNIT), BF16),
            pltpu.VMEM((3, VEC_ROWS, UNIT), BF16),
            pltpu.VMEM((5, VEC_ROWS, UNIT), BF16),
            pltpu.VMEM((4, GVEC_ROWS, UNIT), F32),
            pltpu.VMEM((6, GVEC_ROWS, UNIT), F32),
            dma((24,)),
            dma((images,)),
            dma((RING, 7)),
            dma((RING, 7)),
            dma((RING, 7)),
            dma((RING, 7)),
            dma((4, 4)),
            dma((4, 4)),
            dma((4, images)),
            dma((4, images)),
            dma((5,)),
            dma((5,)),
            dma((6,)),
            dma((6,)),
        ],
        compiler_params=pltpu.CompilerParams(
            collective_id=0, has_side_effects=True, vmem_limit_bytes=64 * 2**20 - 2**16
        ),
        name="layer",
    )(lengths, tok, cot, vec, *weights)
    result, tok_grad, gq, go, g1, g2, gvec = outs

    def unpadded(values):
        return values.reshape(images, R, D)[:, :half]

    def owned(values):
        if linked:
            return values
        flat = values.reshape(D, values.shape[-1]).astype(F32)
        return lax.psum_scatter(flat, "dp", scatter_dimension=0, tiled=True)

    gq, go, g1, g2 = owned(gq), owned(go), owned(g1), owned(g2)
    gq = jnp.swapaxes(gq.reshape(share, heads // 4, 3, 4, HD), 2, 3).reshape(share, heads * 3 * HD)
    if not linked:
        gvec = lax.psum(gvec, "dp")
    norms_grad = own_part(gvec[:24].reshape(6, D), dp, share)
    qv_grad = jnp.swapaxes(gvec[24:28].reshape(4, 2, 2, HD), 1, 2).reshape(heads, 2 * HD)
    qv_grad = own_part(qv_grad, dp, 2 * HD // parts)
    fc1_grad = own_part(gvec[28:36].reshape(-1, 128), dp, 128 // parts)
    return (
        unpadded(result),
        unpadded(tok_grad),
        norms_grad[0],
        norms_grad[1],
        gq,
        qv_grad,
        go,
        norms_grad[2],
        norms_grad[3],
        norms_grad[4],
        g1,
        fc1_grad,
        g2,
        norms_grad[5],
    )


def solution(mesh):
    linked = mesh.shape["dp"] == 16
    vector = P("dp")
    weight = P("dp", "tensor")
    bias = P("tensor", "dp")
    tokens = P("dp", "tensor", None)
    in_specs = (
        tokens,
        vector,
        vector,
        vector,
        weight,
        bias,
        weight,
        vector,
        vector,
        vector,
        weight,
        bias,
        weight,
        vector,
        tokens,
    )
    out_specs = (
        tokens,
        tokens,
        vector,
        vector,
        weight,
        bias,
        weight,
        vector,
        vector,
        vector,
        weight,
        bias,
        weight,
        vector,
    )
    return jax.shard_map(
        functools.partial(body, linked),
        mesh=mesh,
        in_specs=in_specs,
        out_specs=out_specs,
        check_vma=False,
    )
```

time: 1330 us -> 311 us (0.23)
  waiting for transfers between devices: 515 us -> 0 us
  matrix products: 287 us -> 0 us
  Pallas kernels: 0 us -> 285 us
  blocking collectives: 258 us -> 0 us
  other arithmetic: 126 us -> 0.86 us
  local copies, waits for them, and re-layouts: 100 us -> 23.9 us
  between operations: 18.7 us -> 0.85 us
    dot_general x136 -> x0, matrix products: 287 us -> none  [the longest x32 45.4 us: masked_scores(): jnp.einsum('xjz,xez->xje', query_matrix, key_matrix_rows, preferred_eleme...]
    pallas_call x0 -> x1, Pallas kernels: none -> 285 us  [body(): pl.pallas_call(functools.partial(layer_kernel, images, half, R, linked),...]
    unnamed x25 -> x0, waiting for transfers between devices: 217 us -> none
    all_gather x12 -> x0, waiting for transfers between devices: 191 us -> none  [the longest x1 80.4 us: body(): lax.all_gather(fc2_weight, 'dp', axis=0, tiled=True)]
    unnamed x4 -> x0, blocking collectives: 177 us -> none
    reduce_scatter x3 -> x0, waiting for transfers between devices: 107 us -> none  [the longest x1 107 us: body(): lax.psum_scatter(totals[2], 'dp', scatter_dimension=0, tiled=True)]
    all_gather x2 -> x0, blocking collectives: 78 us -> none  [the longest x1 42 us: body(): lax.all_gather(fc1_bias, 'dp', axis=1, tiled=True)]
    unnamed x157 -> x23, local copies, waits for them, and re-layouts: 75.6 us -> 10.6 us
  transfers between devices with their start and end apart: 23 -> 0, of which waited for: 14 -> 0; matrix products, arithmetic and copies ran while one was open for 30% -> 0% of each run, Pallas kernels for 0% -> 0%
where the time goes in v1:
time: 311 us
  Pallas kernels  285 us (92%)
  local copies, waits for them, and re-layouts  23.9 us (8%)
    pallas_call x1, Pallas kernels, body(): pl.pallas_call(functools.partial(layer_kernel, images, half, R, linked),...  285 us
    unnamed x23, local copies, waits for them, and re-layouts  10.6 us

profile of v1, /device:TPU:0, one launch (start us, length us, event | category | flops | bytes accessed | tf_op | source)
XLA Modules:
  0.0 310.8 jit_solution(4430520663820880746)
XLA Ops:
  0.7 0.7 tile.14
  1.9 0.8 copy.41
  2.9 0.8 stack.27
  3.9 0.7 maximum_maximum_fusion.vec_in
  4.6 1.6 copy.51
  6.2 1.1 pad.7.clone
  7.3 0.6 copy-done
  8.2 1.2 pad.8.cot_in
  10.0 0.9 reshape.130.wq_in
  10.9 285.2 %layer.1 = (bf16[608,1024]{1,0:T(8,128)(2,1)}, bf16[608,1024]{1,0:T(8,128)(2,1)}, f32[64,1536]{1,0:T(8,128)}, f32[64,512]{1,0:T(8,128)}, f32[64,2048]{1,0:T(8,12...) custom-call(s32[2]{0:T(128)} %lengths.1, bf16[608,1024]{1,0:T(8,128)(2,1)} %bitcast.33, bf16[2,304,1024]{2,1,0:T(8,128)(2,1)} %pad.8.cot_in, ...), custom_call_target="tpu_custom_call" | custom-call | tf_op jit(solution)/shard_map/layer/pallas_call | solution.py:865
  296.1 0.7 slice.43
  297.0 0.5 slice_bitcast_fusion
  297.5 0.7 slice.46
  298.4 0.7 constant_dynamic-slice_fusion.1
  299.0 0.7 slice.50
  299.8 0.7 copy.50
  300.5 1.4 slice.54
  301.9 2.2 copy.48
  304.2 2.2 copy.49
  306.5 0.4 reshape.134
  307.2 1.4 reshape.135
  308.6 0.7 copy.57
  309.2 0.8 copy.58
  310.0 0.8 copy.59
  (53 shorter events, 2.6 us)
Async XLA Ops:
  6.1 1.7 copy-start
  8.2 1.2 copy-start.5
  301.9 2.3 copy-start.1
  304.2 2.3 copy-start.4
  306.9 1.7 copy-start.6
  307.2 2.0 copy-start.3
  307.2 2.8 copy-start.2

commit v2 on v1

--- a/solution.py
+++ b/solution.py
@@ -10,8 +10,10 @@
 HD = 64
 UNIT = 256
 SLAB = 128
-RING = 4
-BLOCKS = (4, 2, 2)
+LAG = 2
+RING = 2 * LAG + 2
+STEPS = 24 + 4 * LAG
+BLOCKS = (2, 2, 2, 2)
 VEC_ROWS = 48
 GVEC_ROWS = 40
 F32 = jnp.float32
@@ -91,6 +93,7 @@
     r1,
     r2,
     r3,
+    r4,
     vb,
     vbr,
     vs,
@@ -119,18 +122,19 @@
     if linked:
         x = lax.rem(d_idx, 2)
         y = lax.rem(lax.div(d_idx, 2), 2)
-        z = lax.div(d_idx, 4)
-
-        def chip(zz, yy, xx):
-            return {"dp": (zz * 2 + yy) * 2 + xx, "tensor": t_idx}
-
-        xdev = chip(z, y, 1 - x)
-        ydev = chip(z, 1 - y, x)
-        zdev = [chip(lax.rem(z + k, 4), y, x) for k in (1, 2, 3)]
+        b = lax.rem(lax.div(d_idx, 4), 2)
+        a = lax.div(d_idx, 8)
+
+        def chip(aa, bb, yy, xx):
+            return {"dp": ((aa * 2 + bb) * 2 + yy) * 2 + xx, "tensor": t_idx}
+
+        xdev = chip(a, b, y, 1 - x)
+        ydev = chip(a, b, 1 - y, x)
+        bdev = chip(a, 1 - b, y, x)
+        adev = chip(1 - a, b, y, x)
     else:
-        x = y = z = 0
-        xdev = ydev = None
-        zdev = []
+        a = b = y = x = 0
+        xdev = ydev = bdev = adev = None
 
     def remote(src, dst, send, recv, device):
         return pltpu.make_async_remote_copy(
@@ -151,7 +155,7 @@
             copy.wait()
 
     barrier = pltpu.get_barrier_semaphore()
-    peers = [core] + ([xdev, ydev] + zdev if linked else [])
+    peers = [core] + ([xdev, ydev, bdev, adev] if linked else [])
     for peer in peers:
         pl.semaphore_signal(barrier, inc=1, device_id=peer, device_id_type=MESH)
 
@@ -166,7 +170,7 @@
             else (w2_in, s - 16)
         )
         cols = pl.ds(u * UNIT, UNIT)
-        return ref.at[:, cols] if linked else ref.at[:, :, :, :, cols]
+        return ref.at[:, cols] if linked else ref.at[:, :, :, :, :, cols]
 
     def place(s):
         return s + 16 - 16 * (s // 8)
@@ -176,7 +180,7 @@
 
     weight_copies = []
     for s in range(24):
-        target = buf.at[place(s), z, y, x] if linked else buf.at[place(s)]
+        target = buf.at[place(s), a, b, y, x] if linked else buf.at[place(s)]
         weight_copies.append(pltpu.make_async_copy(unit_source(s), target, local_sem.at[s]))
     start(weight_copies)
     cot_copies = [
@@ -186,128 +190,93 @@
     start(cot_copies)
     pl.semaphore_wait(barrier, len(peers))
 
-    def spread1(s):
+    TOP, LOW = pl.ds(0, 32), pl.ds(32, 32)
+
+    def spread(k, s):
         u, slot = place_dyn(s), lax.rem(s, RING)
-        block = buf.at[u, z, y, x]
+        if k == 0:
+            moves = [(buf.at[u, a, b, y, x], adev)]
+        elif k == 1:
+            moves = [(buf.at[u, :, b, y, x, TOP], xdev), (buf.at[u, :, b, y, x, LOW], ydev)]
+        elif k == 2:
+            moves = [(buf.at[u, :, b, y, :, TOP], bdev), (buf.at[u, :, b, :, x, LOW], bdev)]
+        else:
+            moves = [(buf.at[u, :, :, y, :, TOP], ydev), (buf.at[u, :, :, :, x, LOW], xdev)]
         return [
-            remote(block, block, gs.at[slot, k], gr.at[slot, k], zdev[k]) for k in range(3)
-        ]
-
-    def spread2(s):
-        u, slot = place_dyn(s), lax.rem(s, RING)
-        a = buf.at[u, :, y, x, pl.ds(0, 32)]
-        b = buf.at[u, :, y, x, pl.ds(32, 32)]
-        return [
-            remote(a, a, gs.at[slot, 3], gr.at[slot, 3], xdev),
-            remote(b, b, gs.at[slot, 4], gr.at[slot, 4], ydev),
-        ]
-
-    def spread3(s):
-        u, slot = place_dyn(s), lax.rem(s, RING)
-        a = buf.at[u, :, y, :, pl.ds(0, 32)]
-        b = buf.at[u, :, :, x, pl.ds(32, 32)]
-        return [
-            remote(a, a, gs.at[slot, 5], gr.at[slot, 5], ydev),
-            remote(b, b, gs.at[slot, 6], gr.at[slot, 6], xdev),
+            remote(ref, ref, gs.at[slot, 2 * k + n], gr.at[slot, 2 * k + n], device)
+            for n, (ref, device) in enumerate(moves)
         ]
 
     def gather_tick(s):
         if not linked:
             return
         s = jnp.int32(s)
-
-        def begin():
-            start(spread1(s))
-
-        def second():
-            wait(spread1(s - 1))
-            start(spread2(s - 1))
-
-        def third():
-            wait(spread2(s - 2))
-            start(spread3(s - 2))
-
-        def end():
-            wait(spread3(s - 3))
-
-        when(s < 24, begin)
-        when((s >= 1) & (s < 25), second)
-        when((s >= 2) & (s < 26), third)
-        when((s >= 3) & (s < 27), end)
+        when(s < 24, lambda: start(spread(0, s)))
+        for k in range(4):
+            unit = s - (k + 1) * LAG
+
+            def further(k=k, unit=unit):
+                wait(spread(k, unit))
+                if k < 3:
+                    start(spread(k + 1, unit))
+
+            when((unit >= 0) & (unit < 24), further)
+
+    def gather_ticks(low, high):
+        if not linked or low >= high:
+            return
+
+        def one(s, carry):
+            gather_tick(s)
+            return carry
+
+        lax.fori_loop(low, high, one, 0)
 
     def grad_place(r):
         return lax.rem(r + 24, 32)
 
-    def first(r):
+    def collect(k, r):
         g, slot = grad_place(r), lax.rem(r, RING)
+        if k == 0:
+            moves = [
+                (buf.at[g, :, :, 1 - y, :, TOP], r1.at[slot, 0], ydev),
+                (buf.at[g, :, :, :, 1 - x, LOW], r1.at[slot, 1], xdev),
+            ]
+        elif k == 1:
+            moves = [
+                (buf.at[g, :, 1 - b, y, :, TOP], r2.at[slot, 0], bdev),
+                (buf.at[g, :, 1 - b, :, x, LOW], r2.at[slot, 1], bdev),
+            ]
+        elif k == 2:
+            moves = [
+                (buf.at[g, :, b, y, 1 - x, TOP], r3.at[slot, 0], xdev),
+                (buf.at[g, :, b, 1 - y, x, LOW], r3.at[slot, 1], ydev),
+            ]
+        else:
+            moves = [(buf.at[g, 1 - a, b, y, x], r4.at[slot], adev)]
         return [
-            remote(
-                buf.at[g, :, 1 - y, :, pl.ds(0, 32)],
-                r1.at[slot, 0],
-                hs.at[slot, 0],
-                hr.at[slot, 0],
-                ydev,
-            ),
-            remote(
-                buf.at[g, :, :, 1 - x, pl.ds(32, 32)],
-                r1.at[slot, 1],
-                hs.at[slot, 1],
-                hr.at[slot, 1],
-                xdev,
-            ),
+            remote(src, dst, hs.at[slot, 2 * k + n], hr.at[slot, 2 * k + n], device)
+            for n, (src, dst, device) in enumerate(moves)
         ]
 
-    def second_step(r):
+    def add_parts(k, r):
         g, slot = grad_place(r), lax.rem(r, RING)
-        return [
-            remote(
-                buf.at[g, :, y, 1 - x, pl.ds(0, 32)],
-                r2.at[slot, 0],
-                hs.at[slot, 2],
-                hr.at[slot, 2],
-                xdev,
-            ),
-            remote(
-                buf.at[g, :, 1 - y, x, pl.ds(32, 32)],
-                r2.at[slot, 1],
-                hs.at[slot, 3],
-                hr.at[slot, 3],
-                ydev,
-            ),
-        ]
-
-    def third_step(r):
+        if k == 0:
+            top, low, parts = (g, slice(None), slice(None), y, slice(None), TOP), (
+                (g, slice(None), slice(None), slice(None), x, LOW)
+            ), r1
+        elif k == 1:
+            top, low, parts = (g, slice(None), b, y, slice(None), TOP), (
+                (g, slice(None), b, slice(None), x, LOW)
+            ), r2
+        else:
+            top, low, parts = (g, slice(None), b, y, x, TOP), (g, slice(None), b, y, x, LOW), r3
+        buf[top] = (buf[top].astype(F32) + parts[slot, 0].astype(F32)).astype(BF16)
+        buf[low] = (buf[low].astype(F32) + parts[slot, 1].astype(F32)).astype(BF16)
+
+    def add_last(r):
         g, slot = grad_place(r), lax.rem(r, RING)
-        return [
-            remote(
-                buf.at[g, lax.rem(z + k + 1, 4), y, x],
-                r3.at[slot, k],
-                hs.at[slot, 4 + k],
-                hr.at[slot, 4 + k],
-                zdev[k],
-            )
-            for k in range(3)
-        ]
-
-    def add1(r):
-        g, slot = grad_place(r), lax.rem(r, RING)
-        top = buf[g, :, y, :, pl.ds(0, 32)].astype(F32) + r1[slot, 0].astype(F32)
-        buf[g, :, y, :, pl.ds(0, 32)] = top.astype(BF16)
-        low = buf[g, :, :, x, pl.ds(32, 32)].astype(F32) + r1[slot, 1].astype(F32)
-        buf[g, :, :, x, pl.ds(32, 32)] = low.astype(BF16)
-
-    def add2(r):
-        g, slot = grad_place(r), lax.rem(r, RING)
-        top = buf[g, :, y, x, pl.ds(0, 32)].astype(F32) + r2[slot, 0].astype(F32)
-        buf[g, :, y, x, pl.ds(0, 32)] = top.astype(BF16)
-        low = buf[g, :, y, x, pl.ds(32, 32)].astype(F32) + r2[slot, 1].astype(F32)
-        buf[g, :, y, x, pl.ds(32, 32)] = low.astype(BF16)
-
-    def add3(r):
-        g, slot = grad_place(r), lax.rem(r, RING)
-        total = buf[g, z, y, x].astype(F32)
-        for k in range(3):
-            total = total + r3[slot, k].astype(F32)
+        total = buf[g, a, b, y, x].astype(F32) + r4[slot].astype(F32)
 
         def put(ref, base):
             def store():
@@ -324,28 +293,29 @@
         if not linked:
             return
         s = jnp.int32(s)
-
-        def begin():
-            start(first(s))
-
-        def second():
-            wait(first(s - 1))
-            add1(s - 1)
-            start(second_step(s - 1))
-
-        def third():
-            wait(second_step(s - 2))
-            add2(s - 2)
-            start(third_step(s - 2))
-
-        def end():
-            wait(third_step(s - 3))
-            add3(s - 3)
-
-        when((s >= 0) & (s < 24), begin)
-        when((s >= 1) & (s < 25), second)
-        when((s >= 2) & (s < 26), third)
-        when((s >= 3) & (s < 27), end)
+        when((s >= 0) & (s < 24), lambda: start(collect(0, s)))
+        for k in range(4):
+            unit = s - (k + 1) * LAG
+
+            def further(k=k, unit=unit):
+                wait(collect(k, unit))
+                if k < 3:
+                    add_parts(k, unit)
+                    start(collect(k + 1, unit))
+                else:
+                    add_last(unit)
+
+            when((unit >= 0) & (unit < 24), further)
+
+    def scatter_ticks(low, high):
+        if not linked or low >= high:
+            return
+
+        def one(s, carry):
+            scatter_tick(s)
+            return carry
+
+        lax.fori_loop(low, high, one, 0)
 
     def put_grad(r, value):
         buf[grad_place(r)] = value.astype(BF16).reshape(BLOCKS + (D // 16, UNIT))
@@ -355,7 +325,7 @@
                 def store():
                     cols = pl.ds(pl.multiple_of((r - base) * UNIT, UNIT), UNIT)
                     copy = pltpu.make_async_copy(
-                        buf.at[grad_place(r)], ref.at[:, :, :, :, cols], local_sem.at[0]
+                        buf.at[grad_place(r)], ref.at[:, :, :, :, :, cols], local_sem.at[0]
                     )
                     copy.start()
                     copy.wait()
@@ -390,12 +360,11 @@
         return remote(snd.at[j], rcv.at[side, j], xs.at[which, j], xr.at[which, j], core)
 
     def project(which, side, slabs, places, tick=None):
-        groups = len(places)
-
         def one(j, carry):
             left = jnp.concatenate([ref[n] for ref, n in slabs], axis=1)
+            jh, jl = lax.div(j, 2), lax.rem(j, 2)
             right = jnp.concatenate(
-                [buf[u, j].reshape(UNIT, UNIT) for u in places], axis=1
+                [buf[u, jh, jl].reshape(UNIT, UNIT) for u in places], axis=1
             )
             total = mm(left, right, 1, 1)
             for i in range(images):
@@ -406,7 +375,6 @@
                 tick(j)
             return carry
 
-        del groups
         lax.fori_loop(0, D // UNIT, one, 0)
 
     def partial_wait(which, side):
@@ -427,7 +395,7 @@
             body(pl.ds(r, CHUNK), pl.ds(full, CHUNK))
             return carry
 
-        lax.fori_loop(0, R // CHUNK, step, 0, unroll=1)
+        lax.fori_loop(0, R // CHUNK, step, 0, unroll=R // CHUNK)
 
     def tokens_of(i, rows):
         return tok[rows].astype(F32)
@@ -435,27 +403,14 @@
     if linked:
         vb[0] = vec_in[...]
 
-        def vec_copy(k, stage, device):
-            return remote(vb.at[stage], vbr.at[k], vgs.at[k], vgr.at[k], device)
-
-        vx = vec_copy(0, 0, xdev)
-        vx.start()
         wait(weight_copies[:6])
-        gather_tick(0)
-        vx.wait()
-        vb[1] = vb[0] + vbr[0]
-        vy = vec_copy(1, 1, ydev)
-        vy.start()
-        gather_tick(1)
-        vy.wait()
-        vb[2] = vb[1] + vbr[1]
-        vz = [vec_copy(2 + k, 2, zdev[k]) for k in range(3)]
-        start(vz)
-        gather_tick(2)
-        wait(vz)
-        vec[...] = (
-            vb[2].astype(F32) + vbr[2].astype(F32) + vbr[3].astype(F32) + vbr[4].astype(F32)
-        )
+        for k, device in enumerate((adev, xdev, bdev, ydev)):
+            copy = remote(vb.at[k], vbr.at[k], vgs.at[k], vgr.at[k], device)
+            copy.start()
+            gather_tick(k)
+            copy.wait()
+            vb[k + 1] = vb[k] + vbr[k]
+        vec[...] = vb[4].astype(F32)
     else:
         wait(weight_copies[:6])
         vec[...] = vec_in[...].astype(F32)
@@ -476,12 +431,13 @@
 
         token_loop(i, norm_one)
         token_exchange(0, h1, i).start()
+        if i == 0:
+            gather_tick(4)
     wait(weight_copies[6:])
     wait(cot_copies)
     for i in range(images):
         token_exchange(1, cot, i).start()
-    for s in (3, 4, 5):
-        gather_tick(s)
+    gather_ticks(5, 3 + 4 * LAG)
     for i in range(images):
         token_exchange(0, h1, i).wait()
         token_exchange(1, cot, i).wait()
@@ -547,14 +503,15 @@
         project_heads(c)
 
         def attend_step(n, carry):
-            gather_tick(6 + 4 * c + n)
+            if linked:
+                pl.when(n < 3)(lambda: gather_tick(3 + 4 * LAG + 3 * c + n))
             attend(lax.div(n, 2), c, lax.rem(n, 2))
             return carry
 
         lax.fori_loop(0, images * 2, attend_step, 0)
 
     project(0, 0, [(ctx, n) for n in range(4)], [22, 23])
-    gather_tick(14)
+    gather_tick(9 + 4 * LAG)
     partial_wait(0, 0)
     for i in range(images):
 
@@ -567,13 +524,14 @@
         token_loop(i, norm_two)
         token_exchange(2, h2, i).start()
         if i == 0:
-            gather_tick(15)
+            gather_tick(10 + 4 * LAG)
+    gather_tick(11 + 4 * LAG)
     for i in range(images):
         token_exchange(2, h2, i).wait()
 
     def hidden(u, carry):
         if linked:
-            pl.when(lax.rem(u, 2) == 0)(lambda: gather_tick(16 + lax.div(u, 2)))
+            pl.when(lax.rem(u, 2) == 0)(lambda: gather_tick(12 + 4 * LAG + lax.div(u, 2)))
         pre = mm(h2[...], weight(8 + u), 1, 0) + vec[pl.ds(30 + u, 1)]
         sig = 0.5 * jnp.tanh(0.851 * pre) + 0.5
         active = pre * sig
@@ -586,11 +544,12 @@
 
     def hidden_back(u, carry):
         put_grad(u, mm(cot[...], pair(act, u), 0, 0))
-        gather_tick(20 + u)
+        gather_tick(16 + 4 * LAG + u)
         pre_grad = mm(cot[...], weight(u), 1, 0) * pair(gp, u).astype(F32)
         gvec[pl.ds(28 + u, 1)] = jnp.sum(pre_grad, 0, keepdims=True)
         put_pair(gp, u, pre_grad.astype(BF16))
-        scatter_tick(u - 2)
+        if linked:
+            pl.when(lax.rem(u, 2) == 1)(lambda: scatter_tick(lax.div(u, 2)))
         return carry
 
     lax.fori_loop(0, 8, hidden_back, 0)
@@ -604,16 +563,15 @@
 
         return tick
 
-    project(1, 1, [(act, n) for n in range(16)], list(range(8)), odd_tick(6))
+    project(1, 1, [(act, n) for n in range(16)], list(range(8)), odd_tick(4))
 
     def first_grad(u, carry):
         put_grad(8 + u, mm(h2[...], pair(gp, u), 0, 0))
         if linked:
-            pl.when(lax.rem(u, 3) == 2)(lambda: scatter_tick(8 + lax.div(u, 3)))
+            pl.when(lax.rem(u, 4) == 3)(lambda: scatter_tick(6 + lax.div(u, 4)))
         return carry
 
     lax.fori_loop(0, 8, first_grad, 0)
-    scatter_tick(10)
     partial_wait(1, 1)
     for i in range(images):
 
@@ -622,7 +580,7 @@
             result[rows] = total.astype(BF16)
 
         token_loop(i, finish)
-    project(2, 0, [(gp, n) for n in range(16)], list(range(8, 16)), odd_tick(11))
+    project(2, 0, [(gp, n) for n in range(16)], list(range(8, 16)), odd_tick(8))
     partial_wait(2, 0)
 
     def add_rows(n, value):
@@ -645,18 +603,24 @@
         token_loop(i, norm_two_back)
         token_exchange(3, cot, i).start()
         if i == 0:
-            scatter_tick(13)
+            scatter_tick(10)
+    scatter_tick(11)
     for i in range(images):
         token_exchange(3, cot, i).wait()
 
     def out_back(u, carry):
         put_grad(16 + u, mm(cot[...], pair(ctx, u), 0, 0))
+        return carry
+
+    lax.fori_loop(0, 2, out_back, 0)
+    scatter_tick(12)
+
+    def context_back(u, carry):
         value = mm(cot[...], weight(22 + u), 1, 0)
         put_pair(act, 6 + u, value.astype(BF16))
         return carry
 
-    lax.fori_loop(0, 2, out_back, 0)
-    scatter_tick(14)
+    lax.fori_loop(0, 2, context_back, 0)
 
     def attend_back(i, c, p):
         rows = pl.ds(pl.multiple_of(i * 2 * R, 16), 2 * R)
@@ -727,8 +691,7 @@
     for c in range(2):
 
         def attend_back_step(n, carry):
-            if linked:
-                pl.when(n < 3)(lambda: scatter_tick(15 + 3 * c + n))
+            scatter_tick(13 + 4 * c + n)
             attend_back(lax.div(n, 2), c, lax.rem(n, 2))
             return carry
 
@@ -768,25 +731,20 @@
     vs[0] = gvec[...]
     over_core = sum_copy(0, 0, core)
     over_core.start()
-    scatter_tick(25)
     over_core.wait()
     shared = lax.broadcasted_iota(jnp.int32, (GVEC_ROWS, UNIT), 0) < 24
     gathered = vs[0] + jnp.where(shared, vr[0], 0.0)
     if linked:
         vs[1] = gathered
-        over_x = sum_copy(1, 1, xdev)
-        over_x.start()
-        scatter_tick(26)
-        over_x.wait()
-        vs[2] = vs[1] + vr[1]
-        over_y = sum_copy(2, 2, ydev)
-        over_y.start()
-        over_y.wait()
-        vs[3] = vs[2] + vr[2]
-        over_z = [sum_copy(3 + k, 3, zdev[k]) for k in range(3)]
-        start(over_z)
-        wait(over_z)
-        gvec[...] = vs[3] + vr[3] + vr[4] + vr[5]
+        for k, device in enumerate((adev, xdev, bdev, ydev)):
+            copy = sum_copy(k + 1, k + 1, device)
+            copy.start()
+            if k < 3:
+                scatter_tick(25 + k)
+            copy.wait()
+            vs[k + 2] = vs[k + 1] + vr[k + 1]
+        scatter_ticks(28, STEPS)
+        gvec[...] = vs[5]
     else:
         gvec[...] = gathered
 
@@ -888,19 +846,20 @@
             pltpu.VMEM((T, SLAB), F32),
             pltpu.VMEM((VEC_ROWS, UNIT), F32),
             pltpu.VMEM((6, 8, D), F32),
-            pltpu.VMEM((RING, 2, 4, 2, 32, UNIT), BF16),
-            pltpu.VMEM((RING, 2, 4, 32, UNIT), BF16),
-            pltpu.VMEM((RING, 3, 64, UNIT), BF16),
-            pltpu.VMEM((3, VEC_ROWS, UNIT), BF16),
+            pltpu.VMEM((RING, 2, 2, 2, 2, 32, UNIT), BF16),
+            pltpu.VMEM((RING, 2, 2, 2, 32, UNIT), BF16),
+            pltpu.VMEM((RING, 2, 2, 32, UNIT), BF16),
+            pltpu.VMEM((RING, 64, UNIT), BF16),
             pltpu.VMEM((5, VEC_ROWS, UNIT), BF16),
-            pltpu.VMEM((4, GVEC_ROWS, UNIT), F32),
+            pltpu.VMEM((4, VEC_ROWS, UNIT), BF16),
             pltpu.VMEM((6, GVEC_ROWS, UNIT), F32),
+            pltpu.VMEM((5, GVEC_ROWS, UNIT), F32),
             dma((24,)),
             dma((images,)),
-            dma((RING, 7)),
-            dma((RING, 7)),
-            dma((RING, 7)),
-            dma((RING, 7)),
+            dma((RING, 8)),
+            dma((RING, 8)),
+            dma((RING, 8)),
+            dma((RING, 8)),
             dma((4, 4)),
             dma((4, 4)),
             dma((4, images)),

time: 311 us -> 248 us (0.80); the launches traced: 311 us -> 245 us
  Pallas kernels: 285 us -> 219 us
    pallas_call x1, Pallas kernels: 285 us -> 219 us  [body(): pl.pallas_call(functools.partial(layer_kernel, images, half, R, linked),...]
where the time goes in v2:
time: 248 us; the launch traced here: 245 us
  Pallas kernels  219 us (88%)
  local copies, waits for them, and re-layouts  23.9 us (10%)
    pallas_call x1, Pallas kernels, body(): pl.pallas_call(functools.partial(layer_kernel, images, half, R, linked),...  219 us
    unnamed x23, local copies, waits for them, and re-layouts  10.6 us

profile of v2, /device:TPU:0, one launch (start us, length us, event | category | flops | bytes accessed | tf_op | source)
XLA Modules:
  0.0 244.6 jit_solution(1309752206450965410)
XLA Ops:
  0.7 0.7 tile.14
  1.9 0.8 copy.41
  2.9 0.8 stack.27
  3.9 0.7 maximum_maximum_fusion.vec_in
  4.6 1.6 copy.51
  6.2 1.1 pad.7.clone
  7.3 0.6 copy-done
  8.2 1.2 pad.8.cot_in
  10.0 0.9 reshape.130.wq_in
  10.9 218.7 %layer.1 = (bf16[608,1024]{1,0:T(8,128)(2,1)}, bf16[608,1024]{1,0:T(8,128)(2,1)}, f32[64,1536]{1,0:T(8,128)}, f32[64,512]{1,0:T(8,128)}, f32[64,2048]{1,0:T(8,12...) custom-call(s32[2]{0:T(128)} %lengths.1, bf16[608,1024]{1,0:T(8,128)(2,1)} %bitcast.33, bf16[2,304,1024]{2,1,0:T(8,128)(2,1)} %pad.8.cot_in, ...), custom_call_target="tpu_custom_call" | custom-call | tf_op jit(solution)/shard_map/layer/pallas_call | solution.py:823
  229.7 0.7 slice.43
  230.5 0.5 slice_bitcast_fusion
  231.0 0.7 slice.46
  231.9 0.7 constant_dynamic-slice_fusion.1
  232.6 0.7 slice.50
  233.4 0.7 copy.50
  234.0 1.4 slice.54
  235.4 2.2 copy.48
  237.8 2.2 copy.49
  240.0 0.4 reshape.134
  240.7 1.4 reshape.135
  242.1 0.7 copy.57
  242.8 0.8 copy.58
  243.6 0.8 copy.59
  (53 shorter events, 2.6 us)
Async XLA Ops:
  6.1 1.7 copy-start
  8.2 1.2 copy-start.5
  235.4 2.3 copy-start.1
  237.8 2.3 copy-start.4
  240.4 1.7 copy-start.6
  240.7 2.0 copy-start.3
  240.7 2.8 %copy-start.2 = (f32[64,2048]{1,0:T(8,128)S(1)}, f32[64,2048]{1,0:T(8,128)}, u32[]{:S(2)}) copy-start(f32[64,2048]{1,0:T(8,128)} %get-tuple-element.68) | copy-start | bytes 1572868
